TPU v7x, 128 devices: a whole 4x4x4 slice. The times are simulated.
128 devices in a mesh: user: 16 (over y_lo, z, core), item: 8 (over y_hi, x).
Axes of the slice: x: 4, y: 4 (y_hi: 2, y_lo: 2; y = y_hi * 2 + y_lo), z: 4, core: 2. Of those that a mesh axis runs over, the one named last changes fastest.
Arguments:
- confidence: bfloat16 [16384, 65536], P('user', 'item'), may hold values from 0 to 20, as said below
- item_factors: bfloat16 [65536, 128], P(('item', 'user')), may hold values from -6 to 6
- user_factors: float32 [16384, 128], P(('user', 'item')), may hold values from -0.5 to 0.5
- precond: float32 [128, 128], replicated, may hold values from -0.00390625 to 0.5, as said below
Outputs:
- updated_users: float32 [16384, 128], P(('user', 'item'))
Inputs may be any that keep to these rules, and one draw needn't show every extreme that they name: `confidence`: zero or between 1 and 20. `precond`: diagonally dominant with a positive diagonal.
All inputs are finite; a program needn't handle non-finite values.
Results may differ from a plain program's by a relative error of at most 0.0025.
Values may be sent and summed in bfloat16 or wider, within the bound.
A program may use at most 64 MiB of HBM per device.

v0:
```python
import jax
import jax.numpy as jnp
from jax import lax
from jax.sharding import PartitionSpec as P

TURNS = 2


prior_weight = 64.0
gram_coef = 0.5
ridge_coef = 0.1


def shards(confidence, item_factors, user_factors, precond):
    item_count = lax.axis_size("item")
    user_count = lax.axis_size("user")
    all_items = item_factors.shape[0] * user_count * item_count
    gram_matrix = lax.psum(
        jnp.dot(item_factors.T, item_factors, preferred_element_type=jnp.float32), ("user", "item")
    )
    local_weight = jnp.sum(confidence.astype(jnp.float32), axis=1)
    gathered = lax.all_gather(item_factors, "user", axis=0, tiled=True)
    weight = lax.psum_scatter(local_weight, "item", scatter_dimension=0, tiled=True) + prior_weight
    factors = user_factors
    for sweep in range(TURNS):
        rows_bf = lax.all_gather(factors.astype(jnp.bfloat16), "item", axis=0, tiled=True)
        scores = jnp.dot(rows_bf, gathered.T, preferred_element_type=jnp.float32)
        residual = (confidence * (scores - 1.0)).astype(jnp.bfloat16)
        products = lax.psum_scatter(
            jnp.dot(residual, gathered, preferred_element_type=jnp.float32),
            "item",
            scatter_dimension=0,
            tiled=True,
        )
        gradient = products / weight[:, None]
        gradient = gradient + gram_coef / all_items * jnp.dot(
            factors, gram_matrix, precision=lax.Precision.HIGHEST
        )
        gradient = gradient + ridge_coef * factors
        factors = factors - jnp.dot(gradient, precond, precision=lax.Precision.HIGHEST)
    return factors


def solution(mesh):
    return jax.shard_map(
        shards,
        mesh=mesh,
        in_specs=(P("user", "item"), P(("item", "user"), None), P(("user", "item"), None), P()),
        out_specs=P(("user", "item"), None),
        check_vma=False,
    )
```

profile of v0, /device:TPU:0, one launch (start us, length us, event | category | flops | bytes accessed | tf_op | source)
XLA Modules:
  0.0 279.8 jit_solution(953113390216004406)
XLA Ops:
  7.4 0.0 copy-start
  7.4 0.0 all-gather.2.cloned.1.call-start
  7.4 0.7 all-gather.2.cloned.1.call-update
  8.1 0.0 all-reduce.3.cloned.1.call-start
  8.1 1.8 fusion.20
  10.0 0.0 all-reduce.3.cloned.1.call-update
  10.0 0.0 reduce-scatter.3.cloned.1.call-start
  10.1 0.8 convert_element_type.18
  10.9 0.9 copy.8
  11.8 1.2 dynamic-slice
  13.6 35.2 %all_gather.9 = bf16[1024,128]{1,0:T(8,128)(2,1)S(1)} all-gather(bf16[128,128]{1,0:T(8,128)(2,1)S(1)} %convert_element_type.18), channel_id=1, replica_groups=mesh['user'=16,'item'=8] {'item'}, dimensions={0}, use_global_device_ids=true | all-gather | bytes 294912 | tf_op jit(solution)/shard_map/all_gather | solution.py:26
  48.8 0.0 all-gather.2.cloned.1.call-done
  48.8 17.6 %fusion.4 = f32[1024,128]{0,1:T(8,128)} fusion(bf16[8192,128]{1,0:T(8,128)(2,1)} %all-gather.2.cloned.1.call-done, bf16[1024,8192]{1,0:T(8,128)(2,1)} %param.4, bf16[1024,128]{1,0:T(8,128)(2,1)S(1)} %all_gather.9), kind=kOutput, calls=%fused_computation.6 | convolution fusion | flops 4328521728 | bytes 19660800 | tf_op jit(solution)/shard_map/dot_general | solution.py:30
  66.5 0.0 copy-start.1
  66.5 0.0 copy-start.3
  66.5 0.0 reduce-scatter.3.cloned.1.call-update
  66.5 0.0 reduce-scatter.5.cloned.1.call-start
  66.5 7.0 %convert_reduce_fusion = f32[1024]{0:T(1024)S(1)} fusion(bf16[1024,8192]{1,0:T(8,128)(2,1)} %param.4), kind=kLoop, calls=%fused_computation.1 | loop fusion | flops 16776192 | bytes 16781312 | tf_op jit(solution)/shard_map/reduce_sum | solution.py:21
  73.5 23.8 %all-reduce = f32[1024]{0:T(1024)S(1)} all-reduce(f32[1024]{0:T(1024)S(1)} %convert_reduce_fusion), channel_id=3, replica_groups=mesh['user'=16,'item'=8] {'item'}, use_global_device_ids=true, to_apply=%region_2.0.clone | all-reduce | flops 1024 | bytes 8192
  97.4 0.1 dynamic-slice_add_fusion
  97.4 53.9 %all-reduce.3.cloned.1.call-done = f32[128,128]{1,0:T(8,128)} async-done(((f32[128,128]{1,0:T(8,128)}), f32[128,128]{1,0:T(8,128)}) %all-reduce.3.cloned.1.call-update) | async-done | bytes 65552 | tf_op jit(solution)/shard_map/psum | solution.py:18
  151.4 0.0 reduce-scatter.3.cloned.1.call-done
  151.4 0.0 copy-done.1
  151.4 1.2 fusion.16
  152.5 0.0 copy-done
  152.5 0.3 fusion.19
  152.8 34.4 %all_gather.11 = bf16[1024,128]{1,0:T(8,128)(2,1)S(1)} all-gather(bf16[128,128]{1,0:T(8,128)(2,1)S(1)} %get-tuple-element.5), channel_id=1, replica_groups=mesh['user'=16,'item'=8] {'item'}, dimensions={0}, use_global_device_ids=true | all-gather | bytes 294912 | tf_op jit(solution)/shard_map/all_gather | solution.py:26
  187.2 0.0 copy-done.3
  187.3 0.0 copy-start.2
  187.3 14.5 %fusion.2 = f32[1024,128]{0,1:T(8,128)} fusion(bf16[8192,128]{1,0:T(8,128)(2,1)S(1)} %copy-done.3, bf16[1024,8192]{1,0:T(8,128)(2,1)} %param.4, bf16[1024,128]{1,0:T(8,128)(2,1)S(1)} %all_gather.11), kind=kOutput, calls=%fused_computation.5 | convolution fusion | flops 4328521728 | bytes 19660800 | tf_op jit(solution)/shard_map/dot_general | solution.py:30
  201.8 0.0 reduce-scatter.5.cloned.1.call-update
  201.8 68.9 %reduce-scatter.5.cloned.1.call-done = f32[128,128]{0,1:T(8,128)} async-done(((f32[1024,128]{0,1:T(8,128)}), f32[128,128]{0,1:T(8,128)}) %reduce-scatter.5.cloned.1.call-update) | async-done | bytes 65552 | tf_op jit(solution)/shard_map/reduce_scatter | solution.py:29
  270.7 0.8 broadcast_divide_fusion
  271.5 0.1 copy.9
  271.6 0.0 copy-done.2
  271.6 0.2 fusion.13
  271.8 0.8 convolution_subtract_fusion
Async XLA Ops:
  7.4 145.2 %copy-start = (f32[128,128]{1,0:T(8,128)S(1)}, f32[128,128]{1,0:T(8,128)}, u32[]{:S(2)}) copy-start(f32[128,128]{1,0:T(8,128)} %param.7) | copy-start | bytes 196612
  7.4 41.5 %all-gather.2.cloned.1.call-start = ((), (), s32[]{:S(2)}) async-start(), calls=%async_computation.2 | async-start | bytes 2228224 | tf_op jit(solution)/shard_map/all_gather | solution.py:22
  8.1 143.3 %all-reduce.3.cloned.1.call-start = ((), (), s32[]{:S(2)}) async-start(), calls=%async_computation.4 | async-start | bytes 131072 | tf_op jit(solution)/shard_map/psum | solution.py:18
  10.0 141.4 %reduce-scatter.3.cloned.1.call-start = ((), (), s32[]{:S(2)}) async-start(), calls=%async_computation.3 | async-start | bytes 589824 | tf_op jit(solution)/shard_map/reduce_scatter | solution.py:29
  66.5 84.9 %copy-start.1 = (f32[128,128]{1,0:T(8,128)S(1)}, f32[128,128]{1,0:T(8,128)}, u32[]{:S(2)}) copy-start(f32[128,128]{1,0:T(8,128)} %param.6) | copy-start | bytes 196612
  66.5 120.8 %copy-start.3 = (bf16[8192,128]{1,0:T(8,128)(2,1)S(1)}, bf16[8192,128]{1,0:T(8,128)(2,1)}, u32[]{:S(2)}) copy-start(bf16[8192,128]{1,0:T(8,128)(2,1)} %all-gather.2.cloned.1.call-done) | copy-start | bytes 6291460
  66.5 204.2 %reduce-scatter.5.cloned.1.call-start = ((), (), s32[]{:S(2)}) async-start(), calls=%async_computation.5 | async-start | bytes 589824 | tf_op jit(solution)/shard_map/reduce_scatter | solution.py:29
  187.3 84.4 %copy-start.2 = (f32[128,128]{1,0:T(8,128)S(1)}, f32[128,128]{1,0:T(8,128)}, u32[]{:S(2)}) copy-start(f32[128,128]{1,0:T(8,128)} %all-reduce.3.cloned.1.call-done) | copy-start | bytes 196612
Sparse Core Ops, SparseCore 0:
  10.0 36.6 all-gather.1
  66.6 72.5 reduce-scatter.2
  201.9 68.7 reduce-scatter.4
Sparse Core Ops, SparseCore 1:
  13.3 138.0 all-reduce.2
where the time goes:
time: 280 us
  waiting for transfers between devices  124 us (44%)
  blocking collectives  93.5 us (33%)
  matrix products  36.5 us (13%)
  between operations  15.2 us (5%)
  other arithmetic  8.76 us (3%)
    all_gather x2, blocking collectives, shards(): lax.all_gather(factors.astype(jnp.bfloat16), 'item', axis=0, tiled=True)  69.6 us
    reduce_scatter x2, waiting for transfers between devices, shards(): lax.psum_scatter(jnp.dot(residual, gathered, preferred_element_type=jnp.f...  68.9 us
    psum x1, waiting for transfers between devices, shards(): lax.psum(jnp.dot(item_factors.T, item_factors, preferred_element_type=jnp...  53.9 us
    dot_general x2, matrix products, shards(): jnp.dot(residual, gathered, preferred_element_type=jnp.float32)  32.1 us
    unnamed x1, blocking collectives  23.8 us
    reduce_sum x1, other arithmetic, shards(): local_weight = jnp.sum(confidence.astype(jnp.float32), axis=1)  6.99 us
  transfers between devices with their start and end apart: 4, of which 2 were waited for; matrix products, arithmetic and copies ran while one was open for 11% of the time, Pallas kernels for 0%

commit v1 on v0

v1 whole, which is shorter than its diff:
```python
import jax
import jax.numpy as jnp
from jax import lax
from jax.experimental import pallas as pl
from jax.experimental.pallas import tpu as pltpu
from jax.sharding import PartitionSpec as P

K = 128
ITEMS = 65536
prior_weight = 64.0
gram_coef = 0.5
ridge_coef = 0.1

BF = jnp.bfloat16
F32 = jnp.float32
HIGHEST = lax.Precision.HIGHEST
MESH = pl.DeviceIdType.MESH

OWNERS = ((0, 0), (0, 1), (0, 3), (1, 0), (0, 2), (1, 1), (1, 3), (1, 2))
CHIPS = ((0, 0), (1, 0), (0, 1), (0, 3), (0, 2), (1, 1), (1, 3), (1, 2))


def mirrored(table):
    return tuple(table.index((a, (4 - b) % 4)) for a, b in table)


OWNER_BACK = mirrored(OWNERS)
CHIP_BACK = mirrored(CHIPS)

FIRST_ORDER = (7, 5, 6, 3, 4, 1, 2, 0)
SECOND_ORDER = (0, 1, 7, 5, 6, 3, 4, 2)
LATE_CHIP = 4


def kernel(
    conf_hbm, items, users, precond, out,
    conf, table, rows, total, sums, gram, parts, shares, weight_out, weight_in,
    conf_sem, item_send, item_recv, pair_send, pair_recv,
    row_send, row_recv, part_send, part_recv, weight_send, weight_recv,
):
    user = lax.axis_index("user")
    item = lax.axis_index("item")
    core, z, y = user % 2, (user // 2) % 4, user // 8
    x, half = item % 4, item // 4
    pair = (user + 1 - 2 * core, item)

    def owner(k):
        dh, dx = OWNERS[k]
        return (half + dh) % 2 * 4 + (x + dx) % 4

    def chip(j):
        dy, dz = CHIPS[j]
        return (y + dy) % 2 * 4 + (z + dz) % 4

    peers = [(user, owner(k)) for k in range(8)]
    mates = [(chip(j) * 2 + core, item) for j in range(8)]

    barrier = pltpu.get_barrier_semaphore()
    for device in [pair] + peers[1:] + mates[1:]:
        pl.semaphore_signal(barrier, inc=1, device_id=device, device_id_type=MESH)

    def conf_copy(j, k):
        source = conf_hbm.at[
            pl.ds(pl.multiple_of(owner(k) * 128, 128), 128),
            pl.ds(pl.multiple_of(chip(j) * 1024, 1024), 1024),
        ]
        return pltpu.make_async_copy(
            source, conf.at[k, :, pl.ds(j * 1024, 1024)], conf_sem.at[j, k]
        )

    for j in range(8):
        for k in range(8):
            conf_copy(j, k).start()

    mine = pl.ds(pl.multiple_of(core * 512, 512), 512)
    table[0, mine, :] = items[...]
    rows[0, 0] = users[...].astype(BF)
    sums[...] = jnp.zeros_like(sums)

    def row_copy(turn, k):
        back = OWNER_BACK[k]
        return pltpu.make_async_remote_copy(
            src_ref=rows.at[turn, 0], dst_ref=rows.at[turn, back],
            send_sem=row_send.at[turn, k], recv_sem=row_recv.at[turn, back],
            device_id=peers[k], device_id_type=MESH,
        )

    def item_copy(j):
        back = CHIP_BACK[j]
        return pltpu.make_async_remote_copy(
            src_ref=items, dst_ref=table.at[back, mine],
            send_sem=item_send.at[j], recv_sem=item_recv.at[back],
            device_id=mates[j], device_id_type=MESH,
        )

    def pair_copy(j):
        return pltpu.make_async_remote_copy(
            src_ref=items if j == 0 else table.at[j, mine], dst_ref=table.at[j, mine],
            send_sem=pair_send.at[j], recv_sem=pair_recv.at[j],
            device_id=pair, device_id_type=MESH,
        )

    def part_copy(turn, k):
        back = OWNER_BACK[k]
        return pltpu.make_async_remote_copy(
            src_ref=parts.at[turn, k], dst_ref=shares.at[turn, back],
            send_sem=part_send.at[turn, k], recv_sem=part_recv.at[turn, back],
            device_id=peers[k], device_id_type=MESH,
        )

    def weight_copy(k):
        back = OWNER_BACK[k]
        return pltpu.make_async_remote_copy(
            src_ref=weight_out.at[k], dst_ref=weight_in.at[back],
            send_sem=weight_send.at[k], recv_sem=weight_recv.at[back],
            device_id=peers[k], device_id_type=MESH,
        )

    pl.semaphore_wait(barrier, 15)
    pair_copy(0).start()
    for k in range(1, 8):
        row_copy(0, k).start()
    for j in range(1, 8):
        item_copy(j).start()

    def items_of(first, last):
        return table[first:last].reshape((last - first) * 1024, K)

    def products(turn, k0, k1, first, last, weigh):
        users_here = rows[turn, k0:k1].reshape((k1 - k0) * 128, K)
        block = items_of(first, last)
        tile = conf[k0:k1, :, first * 1024:last * 1024].reshape(
            (k1 - k0) * 128, (last - first) * 1024
        ).astype(F32)
        scores = lax.dot_general(
            users_here, block, (((1,), (1,)), ((), ())), preferred_element_type=F32
        )
        residual = (tile * (scores - 1.0)).astype(BF)
        if weigh:
            folded = tile[:, :K]
            for n in range(1, (last - first) * 8):
                folded = folded + tile[:, n * K:(n + 1) * K]
            sums[k0:k1] = sums[k0:k1] + folded.reshape(k1 - k0, 128, K)
        return jnp.dot(residual, block, preferred_element_type=F32)

    def gram_of(first, last):
        block = items_of(first, last)
        return lax.dot_general(
            block, block, (((0,), (0,)), ((), ())), preferred_element_type=F32
        )

    def forward(first, last):
        for j in range(first, last):
            item_copy(CHIP_BACK[j]).wait_recv()
            pair_copy(j).start()

    for k in range(1, 8):
        row_copy(0, OWNER_BACK[k]).wait_recv()
    pair_copy(0).wait_recv()
    for k in range(8):
        conf_copy(0, k).wait()
    total[...] = products(0, 0, 8, 0, 1, True).reshape(8, 128, K)
    gram[...] = gram_of(0, 1)
    forward(1, LATE_CHIP)
    for j in range(1, LATE_CHIP):
        pair_copy(j).wait_recv()
        for k in range(8):
            conf_copy(j, k).wait()
        total[...] = total[...] + products(0, 0, 8, j, j + 1, True).reshape(8, 128, K)
        gram[...] = gram[...] + gram_of(j, j + 1)
    forward(LATE_CHIP, 8)
    for j in range(LATE_CHIP, 8):
        pair_copy(j).wait_recv()
        for k in range(8):
            conf_copy(j, k).wait()
    scaled = (gram[...] + gram_of(LATE_CHIP, 8)) * (gram_coef / ITEMS)
    high = scaled.astype(BF)
    low = (scaled - high.astype(F32)).astype(BF)
    both = jnp.concatenate([high, low], axis=1)

    def gram_rows(turn, k):
        wide = jnp.dot(rows[turn, k], both, preferred_element_type=F32)
        return wide[:, :K] + wide[:, K:]

    def weight_of(k):
        return lax.dot_general(
            jnp.ones((8, K), F32), sums[k], (((1,), (1,)), ((), ())),
            precision=HIGHEST, preferred_element_type=F32,
        )

    own_part = own_gram = own_weight = None
    for k in FIRST_ORDER:
        part = total[k] + products(0, k, k + 1, LATE_CHIP, 8, True)
        if k == 0:
            own_part, own_gram, own_weight = part, gram_rows(0, k), weight_of(k)
        else:
            weight_out[k] = weight_of(k)
            weight_copy(k).start()
            parts[0, k, 0] = part.astype(BF)
            parts[0, k, 1] = gram_rows(0, k).astype(BF)
            part_copy(0, k).start()

    for k in range(1, 8):
        weight_copy(OWNER_BACK[k]).wait_recv()
        own_weight = own_weight + weight_in[k]
    weight = jnp.transpose(jnp.broadcast_to(own_weight[0:1] + prior_weight, (128, K)))

    def step(turn, factors, part, gram_part):
        for k in range(1, 8):
            part_copy(turn, OWNER_BACK[k]).wait_recv()
            part = part + shares[turn, k, 0].astype(F32)
            gram_part = gram_part + shares[turn, k, 1].astype(F32)
        gradient = part / weight + gram_part + ridge_coef * factors
        return factors - jnp.dot(
            gradient, precond[...], precision=HIGHEST, preferred_element_type=F32
        )

    factors = step(0, users[...], own_part, own_gram)
    rows[1, 0] = factors.astype(BF)
    for k in range(1, 8):
        row_copy(1, k).start()

    for k in SECOND_ORDER:
        if k:
            row_copy(1, OWNER_BACK[k]).wait_recv()
        part = products(1, k, k + 1, 0, 8, False)
        if k == 0:
            own_part, own_gram = part, gram_rows(1, k)
        else:
            parts[1, k, 0] = part.astype(BF)
            parts[1, k, 1] = gram_rows(1, k).astype(BF)
            part_copy(1, k).start()
    out[...] = step(1, factors, own_part, own_gram)

    pair_copy(0).wait_send()
    for k in range(1, 8):
        item_copy(k).wait_send()
        pair_copy(k).wait_send()
        weight_copy(k).wait_send()
        for turn in range(2):
            row_copy(turn, k).wait_send()
            part_copy(turn, k).wait_send()


def shards(confidence, item_factors, user_factors, precond):
    vmem = pl.BlockSpec(memory_space=pltpu.VMEM)
    dma = pltpu.SemaphoreType.DMA
    return pl.pallas_call(
        kernel,
        name="user_half_step",
        out_shape=jax.ShapeDtypeStruct(user_factors.shape, F32),
        in_specs=[pl.BlockSpec(memory_space=pl.ANY), vmem, vmem, vmem],
        out_specs=vmem,
        scratch_shapes=[
            pltpu.VMEM((8, 128, 8192), BF),
            pltpu.VMEM((8, 1024, K), BF),
            pltpu.VMEM((2, 8, 128, K), BF),
            pltpu.VMEM((8, 128, K), F32),
            pltpu.VMEM((8, 128, K), F32),
            pltpu.VMEM((K, K), F32),
            pltpu.VMEM((2, 8, 2, 128, K), BF),
            pltpu.VMEM((2, 8, 2, 128, K), BF),
            pltpu.VMEM((8, 8, K), F32),
            pltpu.VMEM((8, 8, K), F32),
            dma((8, 8)), dma((8,)), dma((8,)), dma((8,)), dma((8,)),
            dma((2, 8)), dma((2, 8)), dma((2, 8)), dma((2, 8)), dma((8,)), dma((8,)),
        ],
        compiler_params=pltpu.CompilerParams(
            collective_id=0, has_side_effects=True, vmem_limit_bytes=56 * 2**20
        ),
        cost_estimate=pl.CostEstimate(
            flops=4 * 2 * 1024 * 8192 * 128, bytes_accessed=17 * 2**20, transcendentals=0
        ),
    )(confidence, item_factors, user_factors, precond)


def solution(mesh):
    return jax.shard_map(
        shards,
        mesh=mesh,
        in_specs=(P("user", "item"), P(("item", "user"), None), P(("user", "item"), None), P()),
        out_specs=P(("user", "item"), None),
        check_vma=False,
    )
```

time: 280 us -> 61.4 us (0.22)
  waiting for transfers between devices: 124 us -> 0 us
  blocking collectives: 93.5 us -> 0 us
  Pallas kernels: 0 us -> 59.3 us
  matrix products: 36.5 us -> 0 us
  between operations: 15.2 us -> 0.01 us
  other arithmetic: 8.76 us -> 0 us
    all_gather x2 -> x0, blocking collectives: 69.6 us -> none  [shards(): lax.all_gather(factors.astype(jnp.bfloat16), 'item', axis=0, tiled=True)]
    reduce_scatter x2 -> x0, waiting for transfers between devices: 68.9 us -> none  [shards(): lax.psum_scatter(jnp.dot(residual, gathered, preferred_element_type=jnp.f...]
    pallas_call x0 -> x1, Pallas kernels: none -> 59.3 us  [shards(): pl.pallas_call(kernel, name='user_half_step', out_shape=jax.ShapeDtypeStr...]
    psum x1 -> x0, waiting for transfers between devices: 53.9 us -> none  [shards(): lax.psum(jnp.dot(item_factors.T, item_factors, preferred_element_type=jnp...]
    dot_general x7 -> x0, matrix products: 36.5 us -> none  [the longest x2 32.1 us: shards(): jnp.dot(residual, gathered, preferred_element_type=jnp.float32)]
    unnamed x1 -> x0, blocking collectives: 23.8 us -> none
    reduce_sum x1 -> x0, other arithmetic: 6.99 us -> none  [shards(): local_weight = jnp.sum(confidence.astype(jnp.float32), axis=1)]
  transfers between devices with their start and end apart: 4 -> 0, of which waited for: 2 -> 0; matrix products, arithmetic and copies ran while one was open for 11% -> 0% of each run, Pallas kernels for 0% -> 0%
where the time goes in v1:
time: 61.4 us; the launch traced here: 60.7 us
  Pallas kernels  59.3 us (97%)
  local copies, waits for them, and re-layouts  1.47 us (2%)
    pallas_call x1, Pallas kernels, shards(): pl.pallas_call(kernel, name='user_half_step', out_shape=jax.ShapeDtypeStr...  59.3 us
    unnamed x1, local copies, waits for them, and re-layouts  1.47 us

profile of v1, /device:TPU:0, one launch (start us, length us, event | category | flops | bytes accessed | tf_op | source)
XLA Modules:
  0.0 60.7 jit_solution(2540533401274922738)
XLA Ops:
  0.0 59.3 %user_half_step.1 = f32[128,128]{1,0:T(8,128)} custom-call(bf16[1024,8192]{1,0:T(8,128)(2,1)} %conf_hbm.1, bf16[512,128]{1,0:T(8,128)(2,1)} %items.1, f32[128,128]{1,0:T(8,128)} %users.1, f32[128,128]{1,0:T(8,128)} %precond.1), custom_call_target="tpu_custom_call" | custom-call | flops 8589934592 | bytes 17825792 | tf_op jit(solution)/shard_map/user_half_step/pallas_call | solution.py:248
  59.3 1.5 %copy.6 = f32[128,128]{1,0:T(8,128)} copy(f32[128,128]{1,0:T(8,128)} %user_half_step.1) | data formatting | bytes 131072

commit v2 on v1

v2 whole, which is shorter than its diff:
```python
import jax
import jax.numpy as jnp
from jax import lax
from jax.experimental import pallas as pl
from jax.experimental.pallas import tpu as pltpu
from jax.sharding import PartitionSpec as P

K = 128
ITEMS = 65536
prior_weight = 64.0
gram_coef = 0.5
ridge_coef = 0.1

BF = jnp.bfloat16
F32 = jnp.float32
HIGHEST = lax.Precision.HIGHEST
MESH = pl.DeviceIdType.MESH

OWNERS = ((0, 0), (0, 1), (0, 3), (1, 0), (0, 2), (1, 1), (1, 3), (1, 2))
CHIPS = ((0, 0), (1, 0), (0, 1), (0, 3), (0, 2), (1, 1), (1, 3), (1, 2))


def mirrored(table):
    return tuple(table.index((a, (4 - b) % 4)) for a, b in table)


OWNER_BACK = mirrored(OWNERS)
NEAR = (1, 2, 3, 4)
FAR = (5, 6, 7)
VIA = 3
PASS_ON = {1: 6, 2: 5, 4: 7}
PASSED_BY = {6: 1, 5: 2, 7: 4}
CHIP_BACK = mirrored(CHIPS)

FIRST_ORDER = (7, 5, 6, 3, 4, 1, 2, 0)
SECOND_ORDER = (0, 1, 3, 5, 7, 6, 4, 2)
DIRECT = (1, 2, 3)
FORWARD = (
    (2, 256, 512, 4, 0, 3),
    (3, 0, 256, 4, 4, 2),
    (1, 0, 512, 6, 6, 2),
    (1, 0, 512, 5, 5, 3),
    (4, 0, 512, 7, 7, 1),
)
LATE = 5
GROUPS = ((0, 1), (1, 4), (4, 5), (5, 8))
SOON = 3
SHIFT = 0.1875


def kernel(
    conf_hbm, items_hbm, users_hbm, precond_hbm, out,
    conf, table, users, precond, rows, total, sums, inverse, parts, shares,
    weight_out, weight_in, conf_sem, local_sem, item_send, item_recv, on_send, pair_send,
    pair_recv, row_send, row_recv, part_send, part_recv, weight_send, weight_recv,
    pass_send,
):
    user = lax.axis_index("user")
    item = lax.axis_index("item")
    core, z, y = user % 2, (user // 2) % 4, user // 8
    x, half = item % 4, item // 4
    pair = (user + 1 - 2 * core, item)

    def owner(k):
        dh, dx = OWNERS[k]
        return (half + dh) % 2 * 4 + (x + dx) % 4

    def chip(j):
        dy, dz = CHIPS[j]
        return (y + dy) % 2 * 4 + (z + dz) % 4

    peers = [(user, owner(k)) for k in range(8)]
    mates = [(chip(j) * 2 + core, item) for j in range(8)]

    barrier = pltpu.get_barrier_semaphore()
    greeted = [pair] + [peers[k] for k in NEAR] + [mates[j] for j in DIRECT]
    for device in greeted:
        pl.semaphore_signal(barrier, inc=1, device_id=device, device_id_type=MESH)

    mine = pl.ds(pl.multiple_of(core * 512, 512), 512)
    own_items = pltpu.make_async_copy(items_hbm, table.at[0, mine], local_sem.at[0])
    own_users = pltpu.make_async_copy(users_hbm, users, local_sem.at[1])
    own_precond = pltpu.make_async_copy(precond_hbm, precond, local_sem.at[2])
    own_users.start()
    own_items.start()
    own_precond.start()

    def conf_copy(j, k):
        source = conf_hbm.at[
            pl.ds(pl.multiple_of(owner(k) * 128, 128), 128),
            pl.ds(pl.multiple_of(chip(j) * 1024, 1024), 1024),
        ]
        return pltpu.make_async_copy(
            source, conf.at[k, :, pl.ds(j * 1024, 1024)], conf_sem.at[j, k]
        )

    def load_conf(first, last):
        for j in range(first, last):
            for k in range(8):
                conf_copy(j, k).start()

    load_conf(0, SOON)

    def remote(source, target, send_sem, recv_sem, device):
        return pltpu.make_async_remote_copy(
            src_ref=source, dst_ref=target, send_sem=send_sem, recv_sem=recv_sem,
            device_id=device, device_id_type=MESH,
        )

    def row_copy(turn, k):
        back = OWNER_BACK[k]
        return remote(
            rows.at[turn, 0], rows.at[turn, back],
            row_send.at[turn, k], row_recv.at[turn, back], peers[k],
        )

    def row_pass(k):
        to = PASS_ON[k]
        return remote(
            rows.at[0, VIA], rows.at[0, to], pass_send.at[0, k], row_recv.at[0, to], peers[k]
        )

    def item_copy(j):
        back = CHIP_BACK[j]
        return remote(
            table.at[0, mine], table.at[back, mine], item_send.at[j], item_recv.at[back], mates[j]
        )

    def on_copy(n):
        source, first, last, to, sem, mate = FORWARD[n]
        part = pl.ds(pl.multiple_of(core * 512 + first, 256), last - first)
        return remote(
            table.at[source, part], table.at[to, part],
            on_send.at[n], item_recv.at[sem], mates[mate],
        )

    def pair_copy(g):
        first, last = GROUPS[g]
        return remote(
            table.at[first:last, mine], table.at[first:last, mine],
            pair_send.at[g], pair_recv.at[g], pair,
        )

    def part_copy(turn, k):
        back = OWNER_BACK[k]
        return remote(
            parts.at[turn, k], shares.at[turn, back],
            part_send.at[turn, k], part_recv.at[turn, back], peers[k],
        )

    def weight_copy(k):
        back = OWNER_BACK[k]
        return remote(
            weight_out, weight_in.at[back], weight_send.at[k], weight_recv.at[back], peers[k]
        )

    def weight_pass(k):
        to = PASS_ON[k]
        return remote(
            weight_in.at[VIA], weight_in.at[to], pass_send.at[1, k], weight_recv.at[to], peers[k]
        )

    def add_weights(first, last):
        for j in range(first, last):
            for k in range(8):
                conf_copy(j, k).wait()

            def one(k, carry):
                folded = sums[k]
                for n in range(j * 8, j * 8 + 8):
                    folded = folded + conf[k, :, n * K:(n + 1) * K].astype(F32)
                sums[k] = folded
                return carry

            lax.fori_loop(0, 8, one, 0)

    own_users.wait()
    rows[0, 0] = users[...].astype(BF)
    own_items.wait()
    own_precond.wait()

    pl.semaphore_wait(barrier, len(greeted))
    for k in NEAR:
        row_copy(0, k).start()
    pair_copy(0).start()
    for j in DIRECT[:3]:
        item_copy(j).start()
    load_conf(SOON, 8)
    sums[...] = jnp.zeros_like(sums)
    add_weights(0, SOON)

    def items_of(first, last):
        return table[first:last].reshape((last - first) * 1024, K)

    def products(turn, k0, k1, first, last):
        users_here = rows[turn, k0:k1].reshape((k1 - k0) * 128, K)
        block = items_of(first, last)
        tile = conf[k0:k1, :, first * 1024:last * 1024].reshape(
            (k1 - k0) * 128, (last - first) * 1024
        ).astype(F32)
        scores = lax.dot_general(
            users_here, block, (((1,), (1,)), ((), ())), preferred_element_type=F32
        )
        residual = (tile * (scores - 1.0)).astype(BF)
        done = jnp.dot(residual, block, preferred_element_type=F32)
        return done.reshape(k1 - k0, 128, K)

    def gram_of(first, last):
        block = items_of(first, last)
        return lax.dot_general(
            block, block, (((0,), (0,)), ((), ())), preferred_element_type=F32
        )

    def rows_arrive(turn, *ks):
        for k in ks:
            if turn == 0 and k in FAR:
                row_pass(PASSED_BY[k]).wait_recv()
            else:
                row_copy(turn, OWNER_BACK[k]).wait_recv()

    rows_arrive(0, 1, 2)
    pair_copy(0).wait_recv()
    total[0:3] = products(0, 0, 3, 0, 1)
    rows_arrive(0, VIA)
    for k in PASS_ON:
        row_pass(k).start()
    for j in (2, 3, 1):
        item_copy(CHIP_BACK[j]).wait_recv()
        for n in range(4):
            if FORWARD[n][0] == j:
                on_copy(n).start()
    pair_copy(1).start()

    add_weights(SOON, 8)
    line = lax.broadcasted_iota(jnp.int32, (8, K), 0)
    own_weight = jnp.zeros((8, K), F32)
    for k in range(8):
        summed = lax.dot_general(
            jnp.ones((8, K), F32), sums[k], (((1,), (1,)), ((), ())),
            precision=HIGHEST, preferred_element_type=F32,
        )
        own_weight = jnp.where(line == owner(k), summed, own_weight)
    weight_out[...] = own_weight
    for k in NEAR:
        weight_copy(k).start()

    gram = gram_of(0, 1)
    for n in (0, 1):
        on_copy(n).wait_recv()
    on_copy(4).start()
    pair_copy(2).start()
    pair_copy(1).wait_recv()
    total[0:3] = total[0:3] + products(0, 0, 3, 1, 4)
    rows_arrive(0, *FAR)
    rows_arrive(0, 4)
    weight_copy(OWNER_BACK[VIA]).wait_recv()
    for k in PASS_ON:
        weight_pass(k).start()
    total[3:5] = products(0, 3, 5, 0, 4)
    total[5:8] = products(0, 5, 8, 0, 4)
    for n in (2, 3, 4):
        on_copy(n).wait_recv()
    pair_copy(3).start()
    pair_copy(2).wait_recv()
    total[...] = total[...] + products(0, 0, 8, 4, 5)
    gram = gram + gram_of(1, 5)

    for k in range(1, 8):
        if k in FAR:
            weight_pass(PASSED_BY[k]).wait_recv()
        elif k != VIA:
            weight_copy(OWNER_BACK[k]).wait_recv()
        own_weight = own_weight + weight_in[k]
    reciprocal = 1.0 / (own_weight + prior_weight)
    for k in range(8):
        picked = jnp.sum(jnp.where(line == owner(k), reciprocal, 0.0), axis=0, keepdims=True)
        inverse[k] = jnp.transpose(jnp.broadcast_to(picked, (128, K)))

    pair_copy(3).wait_recv()
    gram = (gram + gram_of(LATE, 8)) * (gram_coef / ITEMS)
    high = gram.astype(BF)
    low = (gram - high.astype(F32)).astype(BF)
    both = jnp.concatenate([high, low], axis=1)

    def part_of(turn, k, product):
        wide = jnp.dot(rows[turn, k], both, preferred_element_type=F32)
        return product * inverse[k] + (wide[:, :K] + wide[:, K:])

    def hand_out(turn, k, product):
        part = part_of(turn, k, product)
        parts[turn, k] = (part - SHIFT * rows[turn, k].astype(F32)).astype(BF)
        part_copy(turn, k).start()

    def step(turn, factors, gradient):
        gradient = gradient + ridge_coef * factors
        gradient = gradient + (7 * SHIFT) * rows[turn, 0].astype(F32)
        for k in FIRST_ORDER[:7]:
            part_copy(turn, OWNER_BACK[k]).wait_recv()
            gradient = gradient + shares[turn, k].astype(F32)
        return factors - jnp.dot(
            gradient, precond[...], precision=HIGHEST, preferred_element_type=F32
        )

    for k in FIRST_ORDER:
        product = total[k] + products(0, k, k + 1, LATE, 8)[0]
        if k:
            hand_out(0, k, product)
        else:
            own = part_of(0, 0, product)
    factors = step(0, users[...], own)
    rows[1, 0] = factors.astype(BF)
    for k in range(1, 8):
        row_copy(1, k).start()

    for k in SECOND_ORDER:
        if k:
            rows_arrive(1, k)
        product = products(1, k, k + 1, 0, 8)[0]
        if k:
            hand_out(1, k, product)
        else:
            own = part_of(1, 0, product)
    out[...] = step(1, factors, own)

    for g in range(len(GROUPS)):
        pair_copy(g).wait_send()
    for j in DIRECT:
        item_copy(j).wait_send()
    for n in range(len(FORWARD)):
        on_copy(n).wait_send()
    for k in PASS_ON:
        row_pass(k).wait_send()
        weight_pass(k).wait_send()
    for k in NEAR:
        weight_copy(k).wait_send()
        row_copy(0, k).wait_send()
    for k in range(1, 8):
        row_copy(1, k).wait_send()
        for turn in range(2):
            part_copy(turn, k).wait_send()


def shards(confidence, item_factors, user_factors, precond):
    dma = pltpu.SemaphoreType.DMA
    return pl.pallas_call(
        kernel,
        name="user_half_step",
        out_shape=jax.ShapeDtypeStruct(user_factors.shape, F32),
        in_specs=[pl.BlockSpec(memory_space=pl.ANY)] * 4,
        out_specs=pl.BlockSpec(memory_space=pltpu.VMEM),
        scratch_shapes=[
            pltpu.VMEM((8, 128, 8192), BF),
            pltpu.VMEM((8, 1024, K), BF),
            pltpu.VMEM((128, K), F32),
            pltpu.VMEM((K, K), F32),
            pltpu.VMEM((2, 8, 128, K), BF),
            pltpu.VMEM((8, 128, K), F32),
            pltpu.VMEM((8, 128, K), F32),
            pltpu.VMEM((8, 128, K), F32),
            pltpu.VMEM((2, 8, 128, K), BF),
            pltpu.VMEM((2, 8, 128, K), BF),
            pltpu.VMEM((8, K), F32),
            pltpu.VMEM((8, 8, K), F32),
            dma((8, 8)), dma((3,)), dma((8,)), dma((8,)), dma((8,)), dma((8,)),
            dma((8,)), dma((2, 8)), dma((2, 8)), dma((2, 8)), dma((2, 8)), dma((8,)), dma((8,)),
            dma((2, 8)),
        ],
        compiler_params=pltpu.CompilerParams(
            collective_id=0, has_side_effects=True, vmem_limit_bytes=56 * 2**20
        ),
        cost_estimate=pl.CostEstimate(
            flops=4 * 2 * 1024 * 8192 * 128, bytes_accessed=17 * 2**20, transcendentals=0
        ),
    )(confidence, item_factors, user_factors, precond)


def solution(mesh):
    return jax.shard_map(
        shards,
        mesh=mesh,
        in_specs=(P("user", "item"), P(("item", "user"), None), P(("user", "item"), None), P()),
        out_specs=P(("user", "item"), None),
        check_vma=False,
    )
```

time: 61.4 us -> 50.7 us (0.83)
  Pallas kernels: 59.3 us -> 49 us
    pallas_call x1, Pallas kernels: 59.3 us -> 49 us  [shards(): pl.pallas_call(kernel, name='user_half_step', out_shape=jax.ShapeDtypeStr...]
where the time goes in v2:
time: 50.7 us; the launch traced here: 50.5 us
  Pallas kernels  49 us (97%)
  local copies, waits for them, and re-layouts  1.47 us (3%)
    pallas_call x1, Pallas kernels, shards(): pl.pallas_call(kernel, name='user_half_step', out_shape=jax.ShapeDtypeStr...  49 us
    unnamed x1, local copies, waits for them, and re-layouts  1.47 us

profile of v2, /device:TPU:0, one launch (start us, length us, event | category | flops | bytes accessed | tf_op | source)
XLA Modules:
  0.0 50.5 jit_solution(12762441802133121819)
XLA Ops:
  0.0 49.0 %user_half_step.1 = f32[128,128]{1,0:T(8,128)} custom-call(bf16[1024,8192]{1,0:T(8,128)(2,1)} %conf_hbm.1, bf16[512,128]{1,0:T(8,128)(2,1)} %items_hbm.1, f32[128,128]{1,0:T(8,128)} %users_hbm.1, f32[128,128]{1,0:T(8,128)} %precond_hbm.1), custom_call_target="tpu_custom_call" | custom-call | flops 8589934592 | bytes 17825792 | tf_op jit(solution)/shard_map/user_half_step/pallas_call | solution.py:345
  49.0 1.5 %copy.6 = f32[128,128]{1,0:T(8,128)} copy(f32[128,128]{1,0:T(8,128)} %user_half_step.1) | data formatting | bytes 131072

commit v3 on v2

--- a/solution.py
+++ b/solution.py
@@ -340,9 +340,13 @@
             part_copy(turn, k).wait_send()
 
 
+def hand_over(result, out):
+    out[...] = result[...]
+
+
 def shards(confidence, item_factors, user_factors, precond):
     dma = pltpu.SemaphoreType.DMA
-    return pl.pallas_call(
+    result = pl.pallas_call(
         kernel,
         name="user_half_step",
         out_shape=jax.ShapeDtypeStruct(user_factors.shape, F32),
@@ -372,6 +376,9 @@
             flops=4 * 2 * 1024 * 8192 * 128, bytes_accessed=17 * 2**20, transcendentals=0
         ),
     )(confidence, item_factors, user_factors, precond)
+    return pl.pallas_call(
+        hand_over, name="hand_over", out_shape=jax.ShapeDtypeStruct(result.shape, F32)
+    )(result)
 
 
 def solution(mesh):

time: 50.7 us -> 50.7 us (level)
  Pallas kernels: 49 us -> 50.5 us
  local copies, waits for them, and re-layouts: 1.47 us -> 0 us
    pallas_call x0 -> x1, Pallas kernels: none -> 1.47 us  [shards(): pl.pallas_call(hand_over, name='hand_over', out_shape=jax.ShapeDtypeStruc...]
    unnamed x1 -> x0, local copies, waits for them, and re-layouts: 1.47 us -> none
where the time goes in v3:
time: 50.7 us; the launch traced here: 50.5 us
  Pallas kernels  50.5 us (100%)
    pallas_call x1, Pallas kernels, shards(): pl.pallas_call(kernel, name='user_half_step', out_shape=jax.ShapeDtypeStr...  49 us
    pallas_call x1, Pallas kernels, shards(): pl.pallas_call(hand_over, name='hand_over', out_shape=jax.ShapeDtypeStruc...  1.47 us

profile of v3, /device:TPU:0, one launch (start us, length us, event | category | flops | bytes accessed | tf_op | source)
XLA Modules:
  0.0 50.5 jit_solution(15546089824524385210)
XLA Ops:
  0.0 49.0 %user_half_step.1.result = f32[128,128]{1,0:T(8,128)} custom-call(bf16[1024,8192]{1,0:T(8,128)(2,1)} %conf_hbm.1, bf16[512,128]{1,0:T(8,128)(2,1)} %items_hbm.1, f32[128,128]{1,0:T(8,128)} %users_hbm.1, f32[128,128]{1,0:T(8,128)} %precond_hbm.1), custom_call_target="tpu_custom_call" | custom-call | flops 8589934592 | bytes 17825792 | tf_op jit(solution)/shard_map/user_half_step/pallas_call | solution.py:349
  49.0 1.5 %hand_over.1 = f32[128,128]{1,0:T(8,128)} custom-call(f32[128,128]{1,0:T(8,128)} %user_half_step.1.result), custom_call_target="tpu_custom_call" | custom-call | tf_op jit(solution)/shard_map/hand_over/pallas_call | solution.py:379
